TPU v7x, 32 devices: a whole 2x2x4 slice. The times are simulated.
32 devices in a mesh: gx: 8 (over z, core), gy: 4 (over y, x).
Axes of the slice: x: 2, y: 2, z: 4, core: 2. Of those that a mesh axis runs over, the one named last changes fastest.
Arguments:
- water_state: float32 [3, 1024, 2048], P(None, 'gy', 'gx'), may hold values from -0.1 to 1, as said below
- ground: float32 [1024, 2048], P('gy', 'gx'), may hold values from 0 to 0.3
- log_rough: float32 [1024, 2048], P('gy', 'gx'), may hold values from -3.5 to -1.6
- moment: float32 [1024, 2048], P('gy', 'gx'), may hold values from -3 to 3
- second: float32 [1024, 2048], P('gy', 'gx'), may hold values from 0.001 to 1
- wet_tiles: int32 [8, 16], P('gy', 'gx'), may hold values from 0 to 1, as said below
- cotangent: float32 [3, 1024, 2048], P(None, 'gy', 'gx'), may hold values from -2400 to 2400
Outputs:
- new_rough: float32 [1024, 2048], P('gy', 'gx')
- new_moment: float32 [1024, 2048], P('gy', 'gx')
- new_second: float32 [1024, 2048], P('gy', 'gx')
Inputs may be any that keep to these rules, and one draw needn't show every extreme that they name: `water_state`: depths (first field) lie in 0.2 to 1.0, discharges in -0.1 to 0.1. `wet_tiles`: two devices of one gy index whose gx indices differ by half of the gx axis form a pair; a pair holds at most 6 wet tiles together, and in every draw some pair holds exactly 6, one of its devices with all its tiles wet.
All inputs are finite; a program needn't handle non-finite values.
Results may differ from a plain program's by a relative error of at most 0.0003.
Values sent between devices are 32-bit elements; how exact they have to be, the bound alone decides.
A program may use at most 64 MiB of HBM per device.

v0:
```python
import functools

import jax
import jax.numpy as jnp
from jax import lax
from jax.experimental import pallas as pl
from jax.experimental.pallas import tpu as pltpu
from jax.sharding import PartitionSpec as P

UPDATES = 20
GRAVITY = 9.81
HALF_STEP = 0.05
GRAVITY_DT = 9.81
SPEED_EPS = 0.0001
BETA_ONE = 0.9
BETA_TWO = 0.999
LEARN_RATE = 0.05
ATAN_SCALE = 1.27

MESH = pl.DeviceIdType.MESH
DEPTHS = (3, 3, 3, 3, 2, 1, 1, 1)
SEAMS = (3, 9, 15, 21, 26, 29, 31, 33)
PACK = 40
FLIP_X = (1, 6)
FLIP_Y = (2, 7)
LANES = 128
SUB = 8
CORNERS = ((-1, -1), (1, -1), (-1, 1), (1, 1))


def before_mask(shape):
    rows = lax.broadcasted_iota(jnp.int32, shape, 0)
    mask = jnp.zeros(shape, jnp.bool_)
    for seam, depth in zip(SEAMS, DEPTHS):
        mask = mask | ((rows >= seam - depth) & (rows < seam))
    return mask


def flip_signs(shape, flipped):
    rows = lax.broadcasted_iota(jnp.int32, shape, 0)
    mask = jnp.zeros(shape, jnp.bool_)
    for field in flipped:
        seam, depth = SEAMS[field], DEPTHS[field]
        mask = mask | ((rows >= seam - depth) & (rows < seam + depth))
    return jnp.where(mask, -1.0, 1.0)


def reflect_rows(src, dst, low, flipped):
    for field, (seam, depth) in enumerate(zip(SEAMS, DEPTHS)):
        sign = -1.0 if field in flipped else 1.0
        for j in range(depth):
            a, b = (seam - 1 - j, seam + j) if low else (seam + j, seam - 1 - j)
            dst[a : a + 1, :] = sign * src[b : b + 1, :]


def flux_parts(depth, east, south):
    inv = 1.0 / depth
    u, v = east * inv, south * inv
    press = (0.5 * GRAVITY) * depth * depth
    qh, qe, qs = 0.25 * depth, 0.25 * east, 0.25 * south
    a0 = HALF_STEP * east
    a1 = HALF_STEP * (east * u + press)
    a2 = HALF_STEP * (east * v)
    b0 = HALF_STEP * south
    b2 = HALF_STEP * (south * v + press)
    return u, v, (qh, qe, qs), (a0, a1, a2), (b0, a2, b2)


def kernel(
    n_gx,
    n_gy,
    water,
    ground,
    rough,
    wet,
    cot,
    grad_out,
    ext,
    rough_v,
    colpk,
    rowpk,
    corpk,
    col_in,
    row_in,
    cor_in,
    slopes,
    mix,
    rise,
    fall,
    state,
    damp,
    vel,
    lam,
    grad,
    load_sem,
    send_sem,
    recv_sem,
):
    side = rough.shape[0]
    width = rough.shape[1]
    tile_rows, tile_cols = wet.shape
    tile_h, tile_w = side // tile_rows, width // tile_cols
    ring = width + LANES
    chunks = side // SUB + 2
    gx = lax.axis_index("gx")
    gy = lax.axis_index("gy")

    def inside(dx, dy):
        checks = []
        if dx < 0:
            checks.append(gx > 0)
        if dx > 0:
            checks.append(gx < n_gx - 1)
        if dy < 0:
            checks.append(gy > 0)
        if dy > 0:
            checks.append(gy < n_gy - 1)
        return functools.reduce(jnp.logical_and, checks)

    def peer(dx, dy):
        return {"gx": gx + dx, "gy": gy + dy}

    loads = [
        pltpu.make_async_copy(water, ext.at[0:3, SUB : SUB + side, 0:width], load_sem.at[0]),
        pltpu.make_async_copy(rough, rough_v, load_sem.at[1]),
        pltpu.make_async_copy(ground, ext.at[3, SUB : SUB + side, 0:width], load_sem.at[2]),
        pltpu.make_async_copy(cot, ext.at[5:8, SUB : SUB + side, 0:width], load_sem.at[3]),
    ]
    for load in loads:
        load.start()

    barrier = pltpu.get_barrier_semaphore()
    around = [(dx, dy) for dx in (-1, 0, 1) for dy in (-1, 0, 1) if (dx, dy) != (0, 0)]
    count = jnp.int32(0)
    for dx, dy in around:
        ok = inside(dx, dy)

        @pl.when(ok)
        def _():
            pl.semaphore_signal(barrier, inc=1, device_id=peer(dx, dy), device_id_type=MESH)

        count = count + ok.astype(jnp.int32)

    for load in loads:
        load.wait()
    for i in range(tile_rows):
        for j in range(tile_cols):
            rs, cs = slice(i * tile_h, (i + 1) * tile_h), slice(j * tile_w, (j + 1) * tile_w)
            coef = GRAVITY_DT * jnp.exp(2.0 * rough_v[rs, cs])
            ext[4, SUB + i * tile_h : SUB + (i + 1) * tile_h, cs] = jnp.where(
                wet[i, j] > 0, coef, -1.0
            )

    for field, (seam, depth) in enumerate(zip(SEAMS, DEPTHS)):
        rowpk[seam - depth : seam, :] = ext[field, SUB + side - depth : SUB + side, 0:width]
        rowpk[seam : seam + depth, :] = ext[field, SUB : SUB + depth, 0:width]
    lane = lax.broadcasted_iota(jnp.int32, (PACK, LANES), 1)
    corpk[...] = jnp.where(lane < LANES // 2, rowpk[:, 0:LANES], rowpk[:, width - LANES : width])
    lane_b = lax.broadcasted_iota(jnp.int32, (LANES, LANES), 1)
    for b in range(side // LANES):
        packed = jnp.zeros((LANES, LANES), jnp.float32)
        rs = slice(SUB + b * LANES, SUB + (b + 1) * LANES)
        for field, (seam, depth) in enumerate(zip(SEAMS, DEPTHS)):
            both = jnp.where(
                lane_b < LANES // 2, ext[field, rs, 0:LANES], ext[field, rs, width - LANES : width]
            )
            both = pltpu.roll(both, seam, 1)
            packed = jnp.where((lane_b >= seam - depth) & (lane_b < seam + depth), both, packed)
        colpk[:, b * LANES : (b + 1) * LANES] = packed.T[0:PACK]

    pl.semaphore_wait(barrier, count)

    def straight(dx, dy, out_slot, in_slot):
        src, dst = (colpk, col_in) if dx else (rowpk, row_in)
        return pltpu.make_async_remote_copy(
            src_ref=src,
            dst_ref=dst.at[in_slot % 2],
            send_sem=send_sem.at[out_slot],
            recv_sem=recv_sem.at[in_slot],
            device_id=peer(dx, dy),
            device_id_type=MESH,
        )

    straights = [(-1, 0, 0, 1), (1, 0, 1, 0), (0, -1, 2, 3), (0, 1, 3, 2)]

    def corner(dx, dy, in_x, in_y, index):
        slot = CORNERS.index((-dx if in_x else dx, -dy if in_y else dy))
        return pltpu.make_async_remote_copy(
            src_ref=corpk,
            dst_ref=cor_in.at[slot],
            send_sem=send_sem.at[4 + index],
            recv_sem=recv_sem.at[4 + slot],
            device_id=peer(dx if in_x else 0, dy if in_y else 0),
            device_id_type=MESH,
        )

    def corner_cases(index):
        dx, dy = CORNERS[index]
        ok_x, ok_y = inside(dx, 0), inside(0, dy)
        no_x, no_y = jnp.logical_not(ok_x), jnp.logical_not(ok_y)
        return [
            (ok_x & ok_y, corner(dx, dy, True, True, index)),
            (ok_x & no_y, corner(dx, dy, True, False, index)),
            (no_x & ok_y, corner(dx, dy, False, True, index)),
        ]

    for args in straights:

        @pl.when(inside(args[0], args[1]))
        def _():
            straight(*args).start()

    for index in range(4):
        for ok, copy in corner_cases(index):

            @pl.when(ok)
            def _():
                copy.start()

        dx, dy = CORNERS[index]

        @pl.when(jnp.logical_not(inside(dx, 0) | inside(0, dy)))
        def _():
            cor_in[index] = corpk[...]

    for slot, (dx, dy) in enumerate(((-1, 0), (1, 0), (0, -1), (0, 1))):

        @pl.when(jnp.logical_not(inside(dx, dy)))
        def _():
            if dx:
                reflect_rows(colpk, col_in.at[slot % 2], dx < 0, FLIP_X)
            else:
                reflect_rows(rowpk, row_in.at[slot % 2], dy < 0, FLIP_Y)

    for args in straights:

        @pl.when(inside(args[0], args[1]))
        def _():
            dx, dy, out_slot, _ = args
            back = straight(dx, dy, out_slot, out_slot)
            back.wait_send()
            back.wait_recv()

    for index in range(4):
        dx, dy = CORNERS[index]

        @pl.when(inside(dx, 0) | inside(0, dy))
        def _():
            copy = pltpu.make_async_remote_copy(
                src_ref=corpk,
                dst_ref=cor_in.at[index],
                send_sem=send_sem.at[4 + index],
                recv_sem=recv_sem.at[4 + index],
                device_id=peer(0, 0),
                device_id_type=MESH,
            )
            copy.wait_send()
            copy.wait_recv()

        @pl.when(jnp.logical_not(inside(0, dy)))
        def _():
            reflect_rows(cor_in.at[index], cor_in.at[index], dy < 0, FLIP_Y)

        @pl.when(jnp.logical_not(inside(dx, 0)))
        def _():
            block = cor_in[index]
            turned = block
            for j in range(max(DEPTHS)):
                if dx < 0:
                    moved = pltpu.roll(block, LANES - 1 - 2 * j, 1)
                    turned = jnp.where(lane == LANES - 1 - j, moved, turned)
                else:
                    moved = pltpu.roll(block, 2 * j + 1, 1)
                    turned = jnp.where(lane == j, moved, turned)
            cor_in[index] = turned * flip_signs((PACK, LANES), FLIP_X)

    low_w = before_mask((PACK, LANES))
    for b in range(side // LANES):
        cs = slice(b * LANES, (b + 1) * LANES)
        halo = jnp.where(low_w, col_in[0, :, cs], col_in[1, :, cs])
        halo = jnp.concatenate([halo, jnp.zeros((LANES - PACK, LANES), jnp.float32)], 0).T
        for field, seam in enumerate(SEAMS):
            ext[field, SUB + b * LANES : SUB + (b + 1) * LANES, width:ring] = pltpu.roll(
                halo, LANES - seam, 1
            )
    for field, (seam, depth) in enumerate(zip(SEAMS, DEPTHS)):
        north, south = slice(seam - depth, seam), slice(seam, seam + depth)
        top, end = slice(SUB - depth, SUB), slice(SUB + side, SUB + side + depth)
        ext[field, top, 0:width] = row_in[0, north, :]
        ext[field, end, 0:width] = row_in[1, south, :]
        east_lane = lax.broadcasted_iota(jnp.int32, (depth, LANES), 1) < LANES // 2
        ext[field, top, width:ring] = jnp.where(east_lane, cor_in[1, north], cor_in[0, north])
        ext[field, end, width:ring] = jnp.where(east_lane, cor_in[3, south], cor_in[2, south])

    def start_of(chunk):
        return chunk * SUB if isinstance(chunk, int) else pl.multiple_of(chunk * SUB, SUB)

    def beside(ref, lead, chunk, shift, columns=slice(None)):
        view = ref.at[lead + (pl.ds(start_of(chunk), 3 * SUB),)]
        return view[SUB + shift : 2 * SUB + shift, columns]

    def east_of(array):
        return pltpu.roll(array, ring - 1, 1)

    def west_of(array):
        return pltpu.roll(array, 1, 1)

    def spread(step, chunk, values):
        at = start_of(chunk)
        u, v, quarter, a, b = flux_parts(*values)
        for f in range(3):
            mix[step, f, pl.ds(at, SUB), :] = east_of(quarter[f] - a[f]) + west_of(quarter[f] + a[f])
            rise[step, f, pl.ds(at + SUB, SUB), :] = quarter[f] - b[f]
            fall[step, f, pl.ds(at + SUB, SUB), :] = quarter[f] + b[f]
        return u, v

    def gather(step, chunk, depth, slope_x, slope_y):
        at = start_of(chunk)
        pre = [
            mix[step, f, pl.ds(at, SUB), :]
            + beside(rise, (step, f), chunk, 1)
            + beside(fall, (step, f), chunk, -1)
            for f in range(3)
        ]
        return pre[0], pre[1] - depth * slope_x, pre[2] - depth * slope_y

    def drag_of(coef, pre):
        depth, east, south = pre
        square = east * east + south * south + SPEED_EPS
        inv_speed = lax.rsqrt(square)
        power = jnp.exp((-7.0 / 3.0) * jnp.log(depth))
        extra = coef * (square * inv_speed) * power
        return extra, 1.0 / (1.0 + extra), inv_speed * inv_speed

    def stage_one(chunk):
        at = start_of(chunk)
        z = ext[3, pl.ds(at, SUB), :]
        scale = HALF_STEP * GRAVITY
        slopes[0, pl.ds(at, SUB), :] = scale * (east_of(z) - west_of(z))
        rise[0, 3, pl.ds(at + SUB, SUB), :] = scale * z
        spread(0, chunk, [ext[f, pl.ds(at, SUB), :] for f in range(3)])

    def stage_two(chunk):
        at = start_of(chunk)
        rows = pl.ds(at, SUB)
        depth, east, south = [ext[f, rows, :] for f in range(3)]
        slope_y = (
            beside(rise, (0, 3), chunk, 1) - beside(rise, (0, 3), chunk, -1)
        )
        slopes[1, rows, :] = slope_y
        pre = gather(0, chunk, depth, slopes[0, rows, :], slope_y)
        coef = ext[4, rows, :]
        is_wet = coef > 0
        extra, inv, _ = drag_of(coef, pre)
        now = [
            jnp.where(is_wet, pre[0], depth),
            jnp.where(is_wet, pre[1] * inv, east),
            jnp.where(is_wet, pre[2] * inv, south),
        ]
        damp[rows, :] = (extra * inv)[:, 0:width]
        for f in range(3):
            state[f, rows, :] = now[f]
        u, v = spread(1, chunk, now)
        vel[0, rows, :] = u[:, 0:width]
        vel[1, rows, :] = v[:, 0:width]

    def stage_three(chunk):
        at = start_of(chunk)
        rows = pl.ds(at, SUB)
        pre = gather(1, chunk, state[0, rows, :], slopes[0, rows, :], slopes[1, rows, :])
        coef = ext[4, rows, :]
        is_wet = coef > 0
        extra, inv, inv_square = drag_of(coef, pre)
        c_depth, c_east, c_south = [ext[5 + f, rows, :] for f in range(3)]
        t = -(c_east * pre[1] + c_south * pre[2]) * (inv * inv * extra)
        lam_rows = pl.ds(at + SUB, SUB)
        tq = t * inv_square
        lam[0, lam_rows, :] = jnp.where(is_wet, c_depth - (7.0 / 3.0) * t / pre[0], 0.0)
        lam[1, lam_rows, :] = jnp.where(is_wet, c_east * inv + tq * pre[1], 0.0)
        lam[2, lam_rows, :] = jnp.where(is_wet, c_south * inv + tq * pre[2], 0.0)
        grad[rows, :] = t[:, 0:width]

    def stage_four(chunk):
        at = start_of(chunk)
        rows = pl.ds(at, SUB)
        mean, dx, dy = [], [], []
        for f in range(3):
            here = lam[f, pl.ds(at + SUB, SUB), :]
            east = east_of(here)[:, 0:width]
            west = west_of(here)[:, 0:width]
            south = beside(lam, (f,), chunk, 1, slice(0, width))
            north = beside(lam, (f,), chunk, -1, slice(0, width))
            if f:
                mean.append(0.25 * ((east + west) + (south + north)))
            dx.append(HALF_STEP * (east - west))
            dy.append(HALF_STEP * (south - north))
        u, v = vel[0, rows, :], vel[1, rows, :]
        cross = dx[2] + dy[1]
        a_east = mean[0] + dx[0] + 2.0 * u * dx[1] + v * cross
        a_south = mean[1] + dy[0] + 2.0 * v * dy[2] + u * cross
        total = grad[rows, :] - (
            a_east * state[1, rows, 0:width] + a_south * state[2, rows, 0:width]
        ) * damp[rows, :]
        is_wet = ext[4, rows, 0:width] > 0
        out = at - SUB if isinstance(chunk, int) else pl.multiple_of(at - SUB, SUB)
        grad_out[pl.ds(out, SUB), :] = jnp.where(is_wet, 2.0 * total, 0.0)

    stages = (
        (6, stage_four, 1, chunks - 1),
        (4, stage_three, 0, chunks),
        (2, stage_two, 0, chunks),
        (0, stage_one, 0, chunks),
    )

    def turn(i):
        for lag, stage, low, high in stages:
            if not isinstance(i, int) or low <= i - lag < high:
                stage(i - lag)

    first = 7
    for i in range(first):
        turn(i)

    def body(i, carry):
        turn(i)
        return carry

    lax.fori_loop(first, chunks, body, 0)
    for i in range(chunks, chunks + 6):
        turn(i)


def on_device(n_gx, n_gy, water_state, ground, log_rough, moment, second, wet_tiles, cotangent):
    side, width = ground.shape
    ring = width + LANES
    rows = side + 2 * SUB
    tall = rows + 2 * SUB
    f32 = jnp.float32
    anywhere = pl.BlockSpec(memory_space=pl.ANY)
    gradient = pl.pallas_call(
        functools.partial(kernel, n_gx, n_gy),
        out_shape=jax.ShapeDtypeStruct((side, width), f32),
        in_specs=[anywhere, anywhere, anywhere, pl.BlockSpec(memory_space=pltpu.SMEM), anywhere],
        out_specs=pl.BlockSpec(memory_space=pltpu.VMEM),
        scratch_shapes=[
            pltpu.VMEM((8, rows, ring), f32),
            pltpu.VMEM((side, width), f32),
            pltpu.VMEM((PACK, side), f32),
            pltpu.VMEM((PACK, width), f32),
            pltpu.VMEM((PACK, LANES), f32),
            pltpu.VMEM((2, PACK, side), f32),
            pltpu.VMEM((2, PACK, width), f32),
            pltpu.VMEM((4, PACK, LANES), f32),
            pltpu.VMEM((2, rows, ring), f32),
            pltpu.VMEM((2, 3, rows, ring), f32),
            pltpu.VMEM((2, 4, tall, ring), f32),
            pltpu.VMEM((2, 3, tall, ring), f32),
            pltpu.VMEM((3, rows, ring), f32),
            pltpu.VMEM((rows, width), f32),
            pltpu.VMEM((2, rows, width), f32),
            pltpu.VMEM((3, tall, ring), f32),
            pltpu.VMEM((rows, width), f32),
            pltpu.SemaphoreType.DMA((4,)),
            pltpu.SemaphoreType.DMA((8,)),
            pltpu.SemaphoreType.DMA((8,)),
        ],
        compiler_params=pltpu.CompilerParams(
            collective_id=0, has_side_effects=True, vmem_limit_bytes=48 * 1024 * 1024
        ),
        name="flood_gradient",
    )(water_state, ground, log_rough, wet_tiles, cotangent)
    new_moment = BETA_ONE * moment + (1.0 - BETA_ONE) * gradient
    new_second = BETA_TWO * second + (1.0 - BETA_TWO) * gradient * gradient
    direction = jnp.arctan2(
        new_moment / (1.0 - BETA_ONE**UPDATES), jnp.sqrt(new_second / (1.0 - BETA_TWO**UPDATES))
    )
    new_rough = log_rough - LEARN_RATE * ATAN_SCALE * direction
    return (new_rough, new_moment, new_second)


def solution(mesh):
    field, plane = P(None, "gy", "gx"), P("gy", "gx")
    return jax.shard_map(
        functools.partial(on_device, mesh.shape["gx"], mesh.shape["gy"]),
        mesh=mesh,
        in_specs=(field, plane, plane, plane, plane, plane, field),
        out_specs=(plane, plane, plane),
        check_vma=False,
    )
```

profile of v0, /device:TPU:0, one launch (start us, length us, event | category | flops | bytes accessed | tf_op | source)
XLA Modules:
  0.0 22.7 jit_solution(8226960939684561938)
XLA Ops:
  0.6 0.0 copy-start
  0.6 0.9 %copy-done = f32[256,256]{1,0:T(8,128)S(1)} copy-done((f32[256,256]{1,0:T(8,128)S(1)}, f32[256,256]{1,0:T(8,128)}, u32[]{:S(2)}) %copy-start) | copy-done | bytes 262168
  1.6 0.0 copy-start.1
  1.6 1.1 %copy-done.1 = f32[3,256,256]{2,1,0:T(8,128)S(1)} copy-done((f32[3,256,256]{2,1,0:T(8,128)S(1)}, f32[3,256,256]{2,1,0:T(8,128)}, u32[]{:S(2)}) %copy-start.1) | copy-done | bytes 786456
  2.7 0.0 copy-start.2
  2.7 1.1 %copy-done.2 = f32[3,256,256]{2,1,0:T(8,128)S(1)} copy-done((f32[3,256,256]{2,1,0:T(8,128)S(1)}, f32[3,256,256]{2,1,0:T(8,128)}, u32[]{:S(2)}) %copy-start.2) | copy-done | bytes 786456
  3.9 0.0 copy-start.3
  3.9 0.9 %copy-done.3 = f32[256,256]{1,0:T(8,128)S(1)} copy-done((f32[256,256]{1,0:T(8,128)S(1)}, f32[256,256]{1,0:T(8,128)}, u32[]{:S(2)}) %copy-start.3) | copy-done | bytes 262168
  4.8 0.0 copy-start.4
  4.8 0.7 %copy-done.4 = s32[2,2]{1,0:T(2,128)S(1)} copy-done((s32[2,2]{1,0:T(2,128)S(1)}, s32[2,2]{1,0:T(2,128)}, u32[]{:S(2)}) %copy-start.4) | copy-done | bytes 40
  5.5 0.0 copy-start.5
  5.5 0.0 copy-start.6
  5.5 15.8 %flood_gradient.1 = f32[256,256]{1,0:T(8,128)S(1)} custom-call(f32[3,256,256]{2,1,0:T(8,128)S(1)} %copy-done.1, f32[256,256]{1,0:T(8,128)S(1)} %copy-done.3, f32[256,256]{1,0:T(8,128)S(1)} %copy-done, s32[2,2]{1,0:T(2,128)S(1)} %copy-done.4, f32[3,256,256]{2,1,0:T(8,128)S(1)} %copy-done.2), custom_call_target="tpu_custom_call" | custom-call | tf_op jit(solution)/shard_map/flood_gradient/pallas_call | solution.py:440
  21.3 0.0 copy-done.5
  21.3 0.0 copy-done.6
  21.3 1.3 %multiply_subtract_fusion = (f32[256,256]{1,0:T(8,128)}, f32[256,256]{1,0:T(8,128)}, f32[256,256]{1,0:T(8,128)}) fusion(f32[256,256]{1,0:T(8,128)S(1)} %copy-done, f32[256,256]{1,0:T(8,128)S(1)} %flood_gradient.1, f32[256,256]{1,0:T(8,128)S(1)} %copy-done.5, f32[256,256]{1,0:T(8,128)S(1)} %copy-done.6), kind=kLoop, calls=%fused_computation.2 | loop fusion | flops 720896 | bytes 1835008 | tf_op jit(solution)/shard_map/sub | solution.py:477
Async XLA Ops:
  0.6 1.0 %copy-start = (f32[256,256]{1,0:T(8,128)S(1)}, f32[256,256]{1,0:T(8,128)}, u32[]{:S(2)}) copy-start(f32[256,256]{1,0:T(8,128)} %rough.1) | copy-start | bytes 786436
  1.6 1.1 %copy-start.1 = (f32[3,256,256]{2,1,0:T(8,128)S(1)}, f32[3,256,256]{2,1,0:T(8,128)}, u32[]{:S(2)}) copy-start(f32[3,256,256]{2,1,0:T(8,128)} %water.1) | copy-start | bytes 2359300
  2.7 1.1 %copy-start.2 = (f32[3,256,256]{2,1,0:T(8,128)S(1)}, f32[3,256,256]{2,1,0:T(8,128)}, u32[]{:S(2)}) copy-start(f32[3,256,256]{2,1,0:T(8,128)} %cot.1) | copy-start | bytes 2359300
  3.9 0.9 %copy-start.3 = (f32[256,256]{1,0:T(8,128)S(1)}, f32[256,256]{1,0:T(8,128)}, u32[]{:S(2)}) copy-start(f32[256,256]{1,0:T(8,128)} %ground.1) | copy-start | bytes 786436
  4.8 0.7 %copy-start.4 = (s32[2,2]{1,0:T(2,128)S(1)}, s32[2,2]{1,0:T(2,128)}, u32[]{:S(2)}) copy-start(s32[2,2]{1,0:T(2,128)} %wet.1) | copy-start | bytes 52
  5.5 15.8 %copy-start.5 = (f32[256,256]{1,0:T(8,128)S(1)}, f32[256,256]{1,0:T(8,128)}, u32[]{:S(2)}) copy-start(f32[256,256]{1,0:T(8,128)} %param.10) | copy-start | bytes 786436
  5.5 15.9 %copy-start.6 = (f32[256,256]{1,0:T(8,128)S(1)}, f32[256,256]{1,0:T(8,128)}, u32[]{:S(2)}) copy-start(f32[256,256]{1,0:T(8,128)} %param.11) | copy-start | bytes 786436
where the time goes:
time: 22.9 us; the launch traced here: 22.7 us
  Pallas kernels  15.8 us (69%)
  local copies, waits for them, and re-layouts  4.84 us (21%)
  other arithmetic  1.31 us (6%)
  between operations  0.67 us (3%)
    pallas_call x1, Pallas kernels, on_device(): pl.pallas_call(functools.partial(kernel, n_gx, n_gy), out_shape=jax.Shape...  15.8 us
    unnamed x14, local copies, waits for them, and re-layouts  4.84 us
    sub x1, other arithmetic, on_device(): new_rough = log_rough - LEARN_RATE * ATAN_SCALE * direction  1.31 us

commit v1 on v0

--- a/solution.py
+++ b/solution.py
@@ -53,8 +53,13 @@
             dst[a : a + 1, :] = sign * src[b : b + 1, :]
 
 
+def inverse(x):
+    guess = pl.reciprocal(x, approx=True)
+    return guess * (2.0 - x * guess)
+
+
 def flux_parts(depth, east, south):
-    inv = 1.0 / depth
+    inv = inverse(depth)
     u, v = east * inv, south * inv
     press = (0.5 * GRAVITY) * depth * depth
     qh, qe, qs = 0.25 * depth, 0.25 * east, 0.25 * south
@@ -72,9 +77,10 @@
     water,
     ground,
     rough,
-    wet,
+    wet_tiles,
     cot,
     grad_out,
+    wet,
     ext,
     rough_v,
     colpk,
@@ -125,6 +131,7 @@
         pltpu.make_async_copy(rough, rough_v, load_sem.at[1]),
         pltpu.make_async_copy(ground, ext.at[3, SUB : SUB + side, 0:width], load_sem.at[2]),
         pltpu.make_async_copy(cot, ext.at[5:8, SUB : SUB + side, 0:width], load_sem.at[3]),
+        pltpu.make_async_copy(wet_tiles, wet, load_sem.at[4]),
     ]
     for load in loads:
         load.start()
@@ -330,7 +337,7 @@
         inv_speed = lax.rsqrt(square)
         power = jnp.exp((-7.0 / 3.0) * jnp.log(depth))
         extra = coef * (square * inv_speed) * power
-        return extra, 1.0 / (1.0 + extra), inv_speed * inv_speed
+        return extra, inverse(1.0 + extra), inv_speed * inv_speed
 
     def stage_one(chunk):
         at = start_of(chunk)
@@ -375,7 +382,7 @@
         t = -(c_east * pre[1] + c_south * pre[2]) * (inv * inv * extra)
         lam_rows = pl.ds(at + SUB, SUB)
         tq = t * inv_square
-        lam[0, lam_rows, :] = jnp.where(is_wet, c_depth - (7.0 / 3.0) * t / pre[0], 0.0)
+        lam[0, lam_rows, :] = jnp.where(is_wet, c_depth - (7.0 / 3.0) * t * inverse(pre[0]), 0.0)
         lam[1, lam_rows, :] = jnp.where(is_wet, c_east * inv + tq * pre[1], 0.0)
         lam[2, lam_rows, :] = jnp.where(is_wet, c_south * inv + tq * pre[2], 0.0)
         grad[rows, :] = t[:, 0:width]
@@ -436,13 +443,14 @@
     rows = side + 2 * SUB
     tall = rows + 2 * SUB
     f32 = jnp.float32
-    anywhere = pl.BlockSpec(memory_space=pl.ANY)
+    in_hbm = pl.BlockSpec(memory_space=pltpu.HBM)
     gradient = pl.pallas_call(
         functools.partial(kernel, n_gx, n_gy),
         out_shape=jax.ShapeDtypeStruct((side, width), f32),
-        in_specs=[anywhere, anywhere, anywhere, pl.BlockSpec(memory_space=pltpu.SMEM), anywhere],
+        in_specs=[in_hbm] * 5,
         out_specs=pl.BlockSpec(memory_space=pltpu.VMEM),
         scratch_shapes=[
+            pltpu.SMEM(wet_tiles.shape, jnp.int32),
             pltpu.VMEM((8, rows, ring), f32),
             pltpu.VMEM((side, width), f32),
             pltpu.VMEM((PACK, side), f32),
@@ -460,12 +468,12 @@
             pltpu.VMEM((2, rows, width), f32),
             pltpu.VMEM((3, tall, ring), f32),
             pltpu.VMEM((rows, width), f32),
-            pltpu.SemaphoreType.DMA((4,)),
+            pltpu.SemaphoreType.DMA((5,)),
             pltpu.SemaphoreType.DMA((8,)),
             pltpu.SemaphoreType.DMA((8,)),
         ],
         compiler_params=pltpu.CompilerParams(
-            collective_id=0, has_side_effects=True, vmem_limit_bytes=48 * 1024 * 1024
+            collective_id=0, has_side_effects=True, vmem_limit_bytes=63 * 1024 * 1024
         ),
         name="flood_gradient",
     )(water_state, ground, log_rough, wet_tiles, cotangent)

time: 22.9 us -> 19.4 us (0.85)
  local copies, waits for them, and re-layouts: 4.84 us -> 0.01 us
  other arithmetic: 1.31 us -> 2.26 us
  Pallas kernels: 15.8 us -> 16.3 us
    unnamed x14 -> x6, local copies, waits for them, and re-layouts: 4.84 us -> 0.01 us
    sub x1, other arithmetic: 1.31 us -> 2.26 us  [on_device(): new_rough = log_rough - LEARN_RATE * ATAN_SCALE * direction]
    pallas_call x1, Pallas kernels: 15.8 us -> 16.3 us  [on_device(): pl.pallas_call(functools.partial(kernel, n_gx, n_gy), out_shape=jax.Shape...]
where the time goes in v1:
time: 19.4 us; the launch traced here: 19.3 us
  Pallas kernels  16.3 us (84%)
  other arithmetic  2.26 us (12%)
  between operations  0.69 us (4%)
    pallas_call x1, Pallas kernels, on_device(): pl.pallas_call(functools.partial(kernel, n_gx, n_gy), out_shape=jax.Shape...  16.3 us
    sub x1, other arithmetic, on_device(): new_rough = log_rough - LEARN_RATE * ATAN_SCALE * direction  2.26 us

profile of v1, /device:TPU:0, one launch (start us, length us, event | category | flops | bytes accessed | tf_op | source)
XLA Modules:
  0.0 19.3 jit_solution(17430634345000760429)
XLA Ops:
  0.6 0.0 copy-start
  0.6 0.0 copy-start.2
  0.7 0.0 copy-start.1
  0.7 16.3 %flood_gradient.1 = f32[256,256]{1,0:T(8,128)} custom-call(f32[3,256,256]{2,1,0:T(8,128)} %water.1, f32[256,256]{1,0:T(8,128)} %ground.1, f32[256,256]{1,0:T(8,128)} %rough.1, s32[2,2]{1,0:T(2,128)} %wet_tiles.1, f32[3,256,256]{2,1,0:T(8,128)} %cot.1), custom_call_target="tpu_custom_call" | custom-call | tf_op jit(solution)/shard_map/flood_gradient/pallas_call | solution.py:447
  17.0 0.0 copy-done
  17.0 0.0 copy-done.2
  17.0 0.0 copy-done.1
  17.0 2.3 %multiply_subtract_fusion = (f32[256,256]{1,0:T(8,128)}, f32[256,256]{1,0:T(8,128)}, f32[256,256]{1,0:T(8,128)}) fusion(f32[256,256]{1,0:T(8,128)S(1)} %copy-done, f32[256,256]{1,0:T(8,128)} %flood_gradient.1, f32[256,256]{1,0:T(8,128)S(1)} %copy-done.1, f32[256,256]{1,0:T(8,128)S(1)} %copy-done.2), kind=kLoop, calls=%fused_computation.2 | loop fusion | flops 720896 | bytes 1835008 | tf_op jit(solution)/shard_map/sub | solution.py:485
Async XLA Ops:
  0.6 16.3 %copy-start = (f32[256,256]{1,0:T(8,128)S(1)}, f32[256,256]{1,0:T(8,128)}, u32[]{:S(2)}) copy-start(f32[256,256]{1,0:T(8,128)} %rough.1) | copy-start | bytes 786436
  0.6 16.3 %copy-start.2 = (f32[256,256]{1,0:T(8,128)S(1)}, f32[256,256]{1,0:T(8,128)}, u32[]{:S(2)}) copy-start(f32[256,256]{1,0:T(8,128)} %param.11) | copy-start | bytes 786436
  0.7 16.3 %copy-start.1 = (f32[256,256]{1,0:T(8,128)S(1)}, f32[256,256]{1,0:T(8,128)}, u32[]{:S(2)}) copy-start(f32[256,256]{1,0:T(8,128)} %param.10) | copy-start | bytes 786436

commit v2 on v1

--- a/solution.py
+++ b/solution.py
@@ -26,14 +26,6 @@
 LANES = 128
 SUB = 8
 CORNERS = ((-1, -1), (1, -1), (-1, 1), (1, 1))
-
-
-def before_mask(shape):
-    rows = lax.broadcasted_iota(jnp.int32, shape, 0)
-    mask = jnp.zeros(shape, jnp.bool_)
-    for seam, depth in zip(SEAMS, DEPTHS):
-        mask = mask | ((rows >= seam - depth) & (rows < seam))
-    return mask
 
 
 def flip_signs(shape, flipped):
@@ -239,6 +231,155 @@
             else:
                 reflect_rows(rowpk, row_in.at[slot % 2], dy < 0, FLIP_Y)
 
+    def beside(ref, lead, at, rows, zone, shift):
+        view = ref.at[lead + (pl.ds(at, rows + 2 * SUB),)]
+        return view[SUB + shift : SUB + rows + shift, zone]
+
+    def east_of(array):
+        return pltpu.roll(array, array.shape[1] - 1, 1)
+
+    def west_of(array):
+        return pltpu.roll(array, 1, 1)
+
+    def spread(step, at, rows, zone, values):
+        here, inner = pl.ds(at, rows), pl.ds(at + SUB, rows)
+        u, v, quarter, a, b = flux_parts(*values)
+        for f in range(3):
+            mix[step, f, here, zone] = east_of(quarter[f] - a[f]) + west_of(quarter[f] + a[f])
+            rise[step, f, inner, zone] = quarter[f] - b[f]
+            fall[step, f, inner, zone] = quarter[f] + b[f]
+        return u, v
+
+    def gather(step, at, rows, zone, depth, slope_x, slope_y):
+        pre = [
+            mix[step, f, pl.ds(at, rows), zone]
+            + beside(rise, (step, f), at, rows, zone, 1)
+            + beside(fall, (step, f), at, rows, zone, -1)
+            for f in range(3)
+        ]
+        return pre[0], pre[1] - depth * slope_x, pre[2] - depth * slope_y
+
+    def drag_of(coef, pre):
+        depth, east, south = pre
+        square = east * east + south * south + SPEED_EPS
+        inv_speed = lax.rsqrt(square)
+        power = jnp.exp((-7.0 / 3.0) * jnp.log(depth))
+        extra = coef * (square * inv_speed) * power
+        return extra, inverse(1.0 + extra), inv_speed * inv_speed
+
+    def stage_one(at, rows, zone):
+        here = pl.ds(at, rows)
+        z = (HALF_STEP * GRAVITY) * ext[3, here, zone]
+        slopes[0, here, zone] = east_of(z) - west_of(z)
+        rise[0, 3, pl.ds(at + SUB, rows), zone] = z
+        spread(0, at, rows, zone, [ext[f, here, zone] for f in range(3)])
+
+    def stage_two(at, rows, zone):
+        here = pl.ds(at, rows)
+        depth, east, south = [ext[f, here, zone] for f in range(3)]
+        slope_y = beside(rise, (0, 3), at, rows, zone, 1) - beside(rise, (0, 3), at, rows, zone, -1)
+        slopes[1, here, zone] = slope_y
+        pre = gather(0, at, rows, zone, depth, slopes[0, here, zone], slope_y)
+        coef = ext[4, here, zone]
+        is_wet = coef > 0
+        extra, inv, _ = drag_of(coef, pre)
+        now = [
+            jnp.where(is_wet, pre[0], depth),
+            jnp.where(is_wet, pre[1] * inv, east),
+            jnp.where(is_wet, pre[2] * inv, south),
+        ]
+        damp[here, zone] = extra * inv
+        for f in range(3):
+            state[f, here, zone] = now[f]
+        u, v = spread(1, at, rows, zone, now)
+        vel[0, here, zone] = u
+        vel[1, here, zone] = v
+
+    def stage_three(at, rows, zone):
+        here = pl.ds(at, rows)
+        pre = gather(1, at, rows, zone, state[0, here, zone], slopes[0, here, zone], slopes[1, here, zone])
+        coef = ext[4, here, zone]
+        is_wet = coef > 0
+        extra, inv, inv_square = drag_of(coef, pre)
+        c_depth, c_east, c_south = [ext[5 + f, here, zone] for f in range(3)]
+        t = -(c_east * pre[1] + c_south * pre[2]) * (inv * inv * extra)
+        inner = pl.ds(at + SUB, rows)
+        tq = t * inv_square
+        lam[0, inner, zone] = jnp.where(is_wet, c_depth - (7.0 / 3.0) * t * inverse(pre[0]), 0.0)
+        lam[1, inner, zone] = jnp.where(is_wet, c_east * inv + tq * pre[1], 0.0)
+        lam[2, inner, zone] = jnp.where(is_wet, c_south * inv + tq * pre[2], 0.0)
+        grad[here, zone] = t
+
+    def stage_four(at, rows, zone):
+        here = pl.ds(at, rows)
+        mean, dx, dy = [], [], []
+        for f in range(3):
+            mid = lam[f, pl.ds(at + SUB, rows), zone]
+            east, west = east_of(mid), west_of(mid)
+            south = beside(lam, (f,), at, rows, zone, 1)
+            north = beside(lam, (f,), at, rows, zone, -1)
+            if f:
+                mean.append(0.25 * ((east + west) + (south + north)))
+            dx.append(HALF_STEP * (east - west))
+            dy.append(HALF_STEP * (south - north))
+        u, v = vel[0, here, zone], vel[1, here, zone]
+        cross = dx[2] + dy[1]
+        a_east = mean[0] + dx[0] + 2.0 * u * dx[1] + v * cross
+        a_south = mean[1] + dy[0] + 2.0 * v * dy[2] + u * cross
+        total = grad[here, zone] - (
+            a_east * state[1, here, zone] + a_south * state[2, here, zone]
+        ) * damp[here, zone]
+        result = jnp.where(ext[4, here, zone] > 0, 2.0 * total, 0.0)
+        if zone is seam_zone:
+            grad[here, zone] = result
+        else:
+            out = at - SUB
+            out = out if isinstance(out, int) else pl.multiple_of(out, SUB)
+            grad_out[pl.ds(out, rows), :] = result
+
+    def run(stages, rows, zone):
+        def turn(i):
+            for lag, stage, low, high in stages:
+                if not isinstance(i, int):
+                    stage(pl.multiple_of((i - lag) * rows, SUB), rows, zone)
+                elif low <= i - lag < high:
+                    stage((i - lag) * rows, rows, zone)
+
+        def body(i, carry):
+            turn(i)
+            return carry
+
+        begin = min(lag + low for lag, _, low, _ in stages)
+        full = max(lag + low for lag, _, low, _ in stages)
+        drain = min(lag + high for lag, _, _, high in stages)
+        end = max(lag + high for lag, _, _, high in stages)
+        for i in range(begin, full):
+            turn(i)
+        lax.fori_loop(full, drain, body, 0)
+        for i in range(drain, end):
+            turn(i)
+
+    main_zone, seam_zone = slice(0, width), slice(width, ring)
+    half, quart = LANES // 2, LANES // 4
+    for b in range(side // LANES):
+        rs = slice(SUB + b * LANES, SUB + (b + 1) * LANES)
+        for field in range(8):
+            ext[field, rs, seam_zone] = jnp.where(
+                lane_b < half,
+                pltpu.roll(ext[field, rs, width - LANES : width], quart, 1),
+                pltpu.roll(ext[field, rs, 0:LANES], LANES - quart, 1),
+            )
+    run(
+        (
+            (6, stage_four, 4, chunks - 4),
+            (4, stage_three, 3, chunks - 3),
+            (2, stage_two, 2, chunks - 2),
+            (0, stage_one, 1, chunks - 1),
+        ),
+        SUB,
+        main_zone,
+    )
+
     for args in straights:
 
         @pl.when(inside(args[0], args[1]))
@@ -281,160 +422,60 @@
                     turned = jnp.where(lane == j, moved, turned)
             cor_in[index] = turned * flip_signs((PACK, LANES), FLIP_X)
 
-    low_w = before_mask((PACK, LANES))
+    gap = jnp.zeros((half - PACK, LANES), jnp.float32)
     for b in range(side // LANES):
         cs = slice(b * LANES, (b + 1) * LANES)
-        halo = jnp.where(low_w, col_in[0, :, cs], col_in[1, :, cs])
-        halo = jnp.concatenate([halo, jnp.zeros((LANES - PACK, LANES), jnp.float32)], 0).T
+        rs = slice(SUB + b * LANES, SUB + (b + 1) * LANES)
+        halo = jnp.concatenate([col_in[1, :, cs], gap, col_in[0, :, cs], gap], 0).T
         for field, seam in enumerate(SEAMS):
-            ext[field, SUB + b * LANES : SUB + (b + 1) * LANES, width:ring] = pltpu.roll(
-                halo, LANES - seam, 1
+            moved = pltpu.roll(halo, (LANES + quart - seam) % LANES, 1)
+            ext[field, rs, seam_zone] = jnp.where(
+                (lane_b >= quart) & (lane_b < LANES - quart), moved, ext[field, rs, seam_zone]
             )
+    for i in range(2):
+        first, last = row_in[i, :, 0:LANES], row_in[i, :, width - LANES : width]
+        west, east = cor_in[2 * i], cor_in[2 * i + 1]
+        cor_in[2 * i] = jnp.where(
+            lane < half,
+            pltpu.roll(jnp.where(lane < half, east, last), quart, 1),
+            pltpu.roll(jnp.where(lane < half, first, west), LANES - quart, 1),
+        )
     for field, (seam, depth) in enumerate(zip(SEAMS, DEPTHS)):
         north, south = slice(seam - depth, seam), slice(seam, seam + depth)
         top, end = slice(SUB - depth, SUB), slice(SUB + side, SUB + side + depth)
-        ext[field, top, 0:width] = row_in[0, north, :]
-        ext[field, end, 0:width] = row_in[1, south, :]
-        east_lane = lax.broadcasted_iota(jnp.int32, (depth, LANES), 1) < LANES // 2
-        ext[field, top, width:ring] = jnp.where(east_lane, cor_in[1, north], cor_in[0, north])
-        ext[field, end, width:ring] = jnp.where(east_lane, cor_in[3, south], cor_in[2, south])
-
-    def start_of(chunk):
-        return chunk * SUB if isinstance(chunk, int) else pl.multiple_of(chunk * SUB, SUB)
-
-    def beside(ref, lead, chunk, shift, columns=slice(None)):
-        view = ref.at[lead + (pl.ds(start_of(chunk), 3 * SUB),)]
-        return view[SUB + shift : 2 * SUB + shift, columns]
-
-    def east_of(array):
-        return pltpu.roll(array, ring - 1, 1)
-
-    def west_of(array):
-        return pltpu.roll(array, 1, 1)
-
-    def spread(step, chunk, values):
-        at = start_of(chunk)
-        u, v, quarter, a, b = flux_parts(*values)
-        for f in range(3):
-            mix[step, f, pl.ds(at, SUB), :] = east_of(quarter[f] - a[f]) + west_of(quarter[f] + a[f])
-            rise[step, f, pl.ds(at + SUB, SUB), :] = quarter[f] - b[f]
-            fall[step, f, pl.ds(at + SUB, SUB), :] = quarter[f] + b[f]
-        return u, v
-
-    def gather(step, chunk, depth, slope_x, slope_y):
-        at = start_of(chunk)
-        pre = [
-            mix[step, f, pl.ds(at, SUB), :]
-            + beside(rise, (step, f), chunk, 1)
-            + beside(fall, (step, f), chunk, -1)
-            for f in range(3)
-        ]
-        return pre[0], pre[1] - depth * slope_x, pre[2] - depth * slope_y
-
-    def drag_of(coef, pre):
-        depth, east, south = pre
-        square = east * east + south * south + SPEED_EPS
-        inv_speed = lax.rsqrt(square)
-        power = jnp.exp((-7.0 / 3.0) * jnp.log(depth))
-        extra = coef * (square * inv_speed) * power
-        return extra, inverse(1.0 + extra), inv_speed * inv_speed
-
-    def stage_one(chunk):
-        at = start_of(chunk)
-        z = ext[3, pl.ds(at, SUB), :]
-        scale = HALF_STEP * GRAVITY
-        slopes[0, pl.ds(at, SUB), :] = scale * (east_of(z) - west_of(z))
-        rise[0, 3, pl.ds(at + SUB, SUB), :] = scale * z
-        spread(0, chunk, [ext[f, pl.ds(at, SUB), :] for f in range(3)])
-
-    def stage_two(chunk):
-        at = start_of(chunk)
-        rows = pl.ds(at, SUB)
-        depth, east, south = [ext[f, rows, :] for f in range(3)]
-        slope_y = (
-            beside(rise, (0, 3), chunk, 1) - beside(rise, (0, 3), chunk, -1)
+        ext[field, top, main_zone] = row_in[0, north, :]
+        ext[field, end, main_zone] = row_in[1, south, :]
+        ext[field, top, seam_zone] = cor_in[0, north, :]
+        ext[field, end, seam_zone] = cor_in[2, south, :]
+
+    for depth, stage in enumerate((stage_one, stage_two, stage_three, stage_four)):
+        low = 1 if stage is stage_four else 0
+        for k in range(depth + 1 - low):
+            stage((k + low) * SUB, SUB, main_zone)
+            stage((chunks - 1 - k - low) * SUB, SUB, main_zone)
+    tall = chunks // 2
+    run(
+        (
+            (6, stage_four, 0, tall),
+            (4, stage_three, 0, tall),
+            (2, stage_two, 0, tall),
+            (0, stage_one, 0, tall),
+        ),
+        2 * SUB,
+        seam_zone,
+    )
+    reach = max(DEPTHS)
+    for b in range(side // LANES):
+        rs = slice(b * LANES, (b + 1) * LANES)
+        found = grad[SUB + b * LANES : SUB + (b + 1) * LANES, seam_zone]
+        grad_out[rs, 0:LANES] = jnp.where(
+            lane_b < reach, pltpu.roll(found, quart, 1), grad_out[rs, 0:LANES]
         )
-        slopes[1, rows, :] = slope_y
-        pre = gather(0, chunk, depth, slopes[0, rows, :], slope_y)
-        coef = ext[4, rows, :]
-        is_wet = coef > 0
-        extra, inv, _ = drag_of(coef, pre)
-        now = [
-            jnp.where(is_wet, pre[0], depth),
-            jnp.where(is_wet, pre[1] * inv, east),
-            jnp.where(is_wet, pre[2] * inv, south),
-        ]
-        damp[rows, :] = (extra * inv)[:, 0:width]
-        for f in range(3):
-            state[f, rows, :] = now[f]
-        u, v = spread(1, chunk, now)
-        vel[0, rows, :] = u[:, 0:width]
-        vel[1, rows, :] = v[:, 0:width]
-
-    def stage_three(chunk):
-        at = start_of(chunk)
-        rows = pl.ds(at, SUB)
-        pre = gather(1, chunk, state[0, rows, :], slopes[0, rows, :], slopes[1, rows, :])
-        coef = ext[4, rows, :]
-        is_wet = coef > 0
-        extra, inv, inv_square = drag_of(coef, pre)
-        c_depth, c_east, c_south = [ext[5 + f, rows, :] for f in range(3)]
-        t = -(c_east * pre[1] + c_south * pre[2]) * (inv * inv * extra)
-        lam_rows = pl.ds(at + SUB, SUB)
-        tq = t * inv_square
-        lam[0, lam_rows, :] = jnp.where(is_wet, c_depth - (7.0 / 3.0) * t * inverse(pre[0]), 0.0)
-        lam[1, lam_rows, :] = jnp.where(is_wet, c_east * inv + tq * pre[1], 0.0)
-        lam[2, lam_rows, :] = jnp.where(is_wet, c_south * inv + tq * pre[2], 0.0)
-        grad[rows, :] = t[:, 0:width]
-
-    def stage_four(chunk):
-        at = start_of(chunk)
-        rows = pl.ds(at, SUB)
-        mean, dx, dy = [], [], []
-        for f in range(3):
-            here = lam[f, pl.ds(at + SUB, SUB), :]
-            east = east_of(here)[:, 0:width]
-            west = west_of(here)[:, 0:width]
-            south = beside(lam, (f,), chunk, 1, slice(0, width))
-            north = beside(lam, (f,), chunk, -1, slice(0, width))
-            if f:
-                mean.append(0.25 * ((east + west) + (south + north)))
-            dx.append(HALF_STEP * (east - west))
-            dy.append(HALF_STEP * (south - north))
-        u, v = vel[0, rows, :], vel[1, rows, :]
-        cross = dx[2] + dy[1]
-        a_east = mean[0] + dx[0] + 2.0 * u * dx[1] + v * cross
-        a_south = mean[1] + dy[0] + 2.0 * v * dy[2] + u * cross
-        total = grad[rows, :] - (
-            a_east * state[1, rows, 0:width] + a_south * state[2, rows, 0:width]
-        ) * damp[rows, :]
-        is_wet = ext[4, rows, 0:width] > 0
-        out = at - SUB if isinstance(chunk, int) else pl.multiple_of(at - SUB, SUB)
-        grad_out[pl.ds(out, SUB), :] = jnp.where(is_wet, 2.0 * total, 0.0)
-
-    stages = (
-        (6, stage_four, 1, chunks - 1),
-        (4, stage_three, 0, chunks),
-        (2, stage_two, 0, chunks),
-        (0, stage_one, 0, chunks),
-    )
-
-    def turn(i):
-        for lag, stage, low, high in stages:
-            if not isinstance(i, int) or low <= i - lag < high:
-                stage(i - lag)
-
-    first = 7
-    for i in range(first):
-        turn(i)
-
-    def body(i, carry):
-        turn(i)
-        return carry
-
-    lax.fori_loop(first, chunks, body, 0)
-    for i in range(chunks, chunks + 6):
-        turn(i)
+        grad_out[rs, width - LANES : width] = jnp.where(
+            lane_b >= LANES - reach,
+            pltpu.roll(found, LANES - quart, 1),
+            grad_out[rs, width - LANES : width],
+        )
 
 
 def on_device(n_gx, n_gy, water_state, ground, log_rough, moment, second, wet_tiles, cotangent):
@@ -464,10 +505,10 @@
             pltpu.VMEM((2, 4, tall, ring), f32),
             pltpu.VMEM((2, 3, tall, ring), f32),
             pltpu.VMEM((3, rows, ring), f32),
-            pltpu.VMEM((rows, width), f32),
-            pltpu.VMEM((2, rows, width), f32),
+            pltpu.VMEM((rows, ring), f32),
+            pltpu.VMEM((2, rows, ring), f32),
             pltpu.VMEM((3, tall, ring), f32),
-            pltpu.VMEM((rows, width), f32),
+            pltpu.VMEM((rows, ring), f32),
             pltpu.SemaphoreType.DMA((5,)),
             pltpu.SemaphoreType.DMA((8,)),
             pltpu.SemaphoreType.DMA((8,)),

time: 19.4 us -> 16.3 us (0.84)
  Pallas kernels: 16.3 us -> 13.2 us
    pallas_call x1, Pallas kernels: 16.3 us -> 13.2 us  [on_device(): pl.pallas_call(functools.partial(kernel, n_gx, n_gy), out_shape=jax.Shape...]
where the time goes in v2:
time: 16.3 us; the launch traced here: 16.2 us
  Pallas kernels  13.2 us (81%)
  other arithmetic  2.26 us (14%)
  between operations  0.69 us (4%)
    pallas_call x1, Pallas kernels, on_device(): pl.pallas_call(functools.partial(kernel, n_gx, n_gy), out_shape=jax.Shape...  13.2 us
    sub x1, other arithmetic, on_device(): new_rough = log_rough - LEARN_RATE * ATAN_SCALE * direction  2.26 us

profile of v2, /device:TPU:0, one launch (start us, length us, event | category | flops | bytes accessed | tf_op | source)
XLA Modules:
  0.0 16.2 jit_solution(9416810380119274279)
XLA Ops:
  0.6 0.0 copy-start
  0.6 0.0 copy-start.2
  0.7 0.0 copy-start.1
  0.7 13.2 %flood_gradient.1 = f32[256,256]{1,0:T(8,128)} custom-call(f32[3,256,256]{2,1,0:T(8,128)} %water.1, f32[256,256]{1,0:T(8,128)} %ground.1, f32[256,256]{1,0:T(8,128)} %rough.1, s32[2,2]{1,0:T(2,128)} %wet_tiles.1, f32[3,256,256]{2,1,0:T(8,128)} %cot.1), custom_call_target="tpu_custom_call" | custom-call | tf_op jit(solution)/shard_map/flood_gradient/pallas_call | solution.py:488
  13.9 0.0 copy-done
  13.9 0.0 copy-done.2
  13.9 0.0 copy-done.1
  13.9 2.3 %multiply_subtract_fusion = (f32[256,256]{1,0:T(8,128)}, f32[256,256]{1,0:T(8,128)}, f32[256,256]{1,0:T(8,128)}) fusion(f32[256,256]{1,0:T(8,128)S(1)} %copy-done, f32[256,256]{1,0:T(8,128)} %flood_gradient.1, f32[256,256]{1,0:T(8,128)S(1)} %copy-done.1, f32[256,256]{1,0:T(8,128)S(1)} %copy-done.2), kind=kLoop, calls=%fused_computation.2 | loop fusion | flops 720896 | bytes 1835008 | tf_op jit(solution)/shard_map/sub | solution.py:526
Async XLA Ops:
  0.6 13.2 %copy-start = (f32[256,256]{1,0:T(8,128)S(1)}, f32[256,256]{1,0:T(8,128)}, u32[]{:S(2)}) copy-start(f32[256,256]{1,0:T(8,128)} %rough.1) | copy-start | bytes 786436
  0.6 13.2 %copy-start.2 = (f32[256,256]{1,0:T(8,128)S(1)}, f32[256,256]{1,0:T(8,128)}, u32[]{:S(2)}) copy-start(f32[256,256]{1,0:T(8,128)} %param.11) | copy-start | bytes 786436
  0.7 13.2 %copy-start.1 = (f32[256,256]{1,0:T(8,128)S(1)}, f32[256,256]{1,0:T(8,128)}, u32[]{:S(2)}) copy-start(f32[256,256]{1,0:T(8,128)} %param.10) | copy-start | bytes 786436

commit v3 on v2

--- a/solution.py
+++ b/solution.py
@@ -21,6 +21,7 @@
 DEPTHS = (3, 3, 3, 3, 2, 1, 1, 1)
 SEAMS = (3, 9, 15, 21, 26, 29, 31, 33)
 PACK = 40
+LIMIT = 62
 FLIP_X = (1, 6)
 FLIP_Y = (2, 7)
 LANES = 128
@@ -150,11 +151,6 @@
                 wet[i, j] > 0, coef, -1.0
             )
 
-    for field, (seam, depth) in enumerate(zip(SEAMS, DEPTHS)):
-        rowpk[seam - depth : seam, :] = ext[field, SUB + side - depth : SUB + side, 0:width]
-        rowpk[seam : seam + depth, :] = ext[field, SUB : SUB + depth, 0:width]
-    lane = lax.broadcasted_iota(jnp.int32, (PACK, LANES), 1)
-    corpk[...] = jnp.where(lane < LANES // 2, rowpk[:, 0:LANES], rowpk[:, width - LANES : width])
     lane_b = lax.broadcasted_iota(jnp.int32, (LANES, LANES), 1)
     for b in range(side // LANES):
         packed = jnp.zeros((LANES, LANES), jnp.float32)
@@ -203,7 +199,18 @@
             (no_x & ok_y, corner(dx, dy, False, True, index)),
         ]
 
-    for args in straights:
+    for args in straights[:2]:
+
+        @pl.when(inside(args[0], args[1]))
+        def _():
+            straight(*args).start()
+
+    for field, (seam, depth) in enumerate(zip(SEAMS, DEPTHS)):
+        rowpk[seam - depth : seam, :] = ext[field, SUB + side - depth : SUB + side, 0:width]
+        rowpk[seam : seam + depth, :] = ext[field, SUB : SUB + depth, 0:width]
+    lane = lax.broadcasted_iota(jnp.int32, (PACK, LANES), 1)
+    corpk[...] = jnp.where(lane < LANES // 2, rowpk[:, 0:LANES], rowpk[:, width - LANES : width])
+    for args in straights[2:]:
 
         @pl.when(inside(args[0], args[1]))
         def _():
@@ -487,7 +494,7 @@
     in_hbm = pl.BlockSpec(memory_space=pltpu.HBM)
     gradient = pl.pallas_call(
         functools.partial(kernel, n_gx, n_gy),
-        out_shape=jax.ShapeDtypeStruct((side, width), f32),
+        out_shape=pltpu.VMEM((side, width), f32),
         in_specs=[in_hbm] * 5,
         out_specs=pl.BlockSpec(memory_space=pltpu.VMEM),
         scratch_shapes=[
@@ -514,7 +521,7 @@
             pltpu.SemaphoreType.DMA((8,)),
         ],
         compiler_params=pltpu.CompilerParams(
-            collective_id=0, has_side_effects=True, vmem_limit_bytes=63 * 1024 * 1024
+            collective_id=0, has_side_effects=True, vmem_limit_bytes=LIMIT * 1024 * 1024
         ),
         name="flood_gradient",
     )(water_state, ground, log_rough, wet_tiles, cotangent)

time: 16.3 us -> 14.7 us (0.902)
  other arithmetic: 2.26 us -> 1.31 us
  Pallas kernels: 13.2 us -> 12.5 us
    sub x1, other arithmetic: 2.26 us -> 1.31 us  [on_device(): new_rough = log_rough - LEARN_RATE * ATAN_SCALE * direction]
    pallas_call x1, Pallas kernels: 13.2 us -> 12.5 us  [on_device(): pl.pallas_call(functools.partial(kernel, n_gx, n_gy), out_shape=pltpu.VME...]
where the time goes in v3:
time: 14.7 us; the launch traced here: 14.5 us
  Pallas kernels  12.5 us (85%)
  other arithmetic  1.31 us (9%)
  between operations  0.69 us (5%)
    pallas_call x1, Pallas kernels, on_device(): pl.pallas_call(functools.partial(kernel, n_gx, n_gy), out_shape=pltpu.VME...  12.5 us
    sub x1, other arithmetic, on_device(): new_rough = log_rough - LEARN_RATE * ATAN_SCALE * direction  1.31 us

profile of v3, /device:TPU:0, one launch (start us, length us, event | category | flops | bytes accessed | tf_op | source)
XLA Modules:
  0.0 14.5 jit_solution(13528787586058729292)
XLA Ops:
  0.6 0.0 copy-start
  0.6 0.0 copy-start.2
  0.7 0.0 copy-start.1
  0.7 12.5 %flood_gradient.1 = f32[256,256]{1,0:T(8,128)S(1)} custom-call(f32[3,256,256]{2,1,0:T(8,128)} %water.1, f32[256,256]{1,0:T(8,128)} %ground.1, f32[256,256]{1,0:T(8,128)} %rough.1, s32[2,2]{1,0:T(2,128)} %wet_tiles.1, f32[3,256,256]{2,1,0:T(8,128)} %cot.1), custom_call_target="tpu_custom_call" | custom-call | tf_op jit(solution)/shard_map/flood_gradient/pallas_call | solution.py:495
  13.2 0.0 copy-done
  13.2 0.0 copy-done.2
  13.2 0.0 copy-done.1
  13.2 1.3 %multiply_subtract_fusion = (f32[256,256]{1,0:T(8,128)}, f32[256,256]{1,0:T(8,128)}, f32[256,256]{1,0:T(8,128)}) fusion(f32[256,256]{1,0:T(8,128)S(1)} %copy-done, f32[256,256]{1,0:T(8,128)S(1)} %flood_gradient.1, f32[256,256]{1,0:T(8,128)S(1)} %copy-done.1, f32[256,256]{1,0:T(8,128)S(1)} %copy-done.2), kind=kLoop, calls=%fused_computation.2 | loop fusion | flops 720896 | bytes 1835008 | tf_op jit(solution)/shard_map/sub | solution.py:533
Async XLA Ops:
  0.6 12.6 %copy-start = (f32[256,256]{1,0:T(8,128)S(1)}, f32[256,256]{1,0:T(8,128)}, u32[]{:S(2)}) copy-start(f32[256,256]{1,0:T(8,128)} %rough.1) | copy-start | bytes 786436
  0.6 12.6 %copy-start.2 = (f32[256,256]{1,0:T(8,128)S(1)}, f32[256,256]{1,0:T(8,128)}, u32[]{:S(2)}) copy-start(f32[256,256]{1,0:T(8,128)} %param.11) | copy-start | bytes 786436
  0.7 12.6 %copy-start.1 = (f32[256,256]{1,0:T(8,128)S(1)}, f32[256,256]{1,0:T(8,128)}, u32[]{:S(2)}) copy-start(f32[256,256]{1,0:T(8,128)} %param.10) | copy-start | bytes 786436

commit v4 on v3

--- a/solution.py
+++ b/solution.py
@@ -352,8 +352,9 @@
                 elif low <= i - lag < high:
                     stage((i - lag) * rows, rows, zone)
 
-        def body(i, carry):
-            turn(i)
+        def body(j, carry):
+            turn(full + 2 * j)
+            turn(full + 2 * j + 1)
             return carry
 
         begin = min(lag + low for lag, _, low, _ in stages)
@@ -362,8 +363,9 @@
         end = max(lag + high for lag, _, _, high in stages)
         for i in range(begin, full):
             turn(i)
-        lax.fori_loop(full, drain, body, 0)
-        for i in range(drain, end):
+        pairs = (drain - full) // 2
+        lax.fori_loop(0, pairs, body, 0)
+        for i in range(full + 2 * pairs, end):
             turn(i)
 
     main_zone, seam_zone = slice(0, width), slice(width, ring)

time: 14.7 us -> 14.7 us (level)
  no operation moved by 1% of the time
where the time goes in v4:
time: 14.7 us; the launch traced here: 14.5 us
  Pallas kernels  12.5 us (85%)
  other arithmetic  1.31 us (9%)
  between operations  0.69 us (5%)
    pallas_call x1, Pallas kernels, on_device(): pl.pallas_call(functools.partial(kernel, n_gx, n_gy), out_shape=pltpu.VME...  12.5 us
    sub x1, other arithmetic, on_device(): new_rough = log_rough - LEARN_RATE * ATAN_SCALE * direction  1.31 us

profile of v4, /device:TPU:0, one launch (start us, length us, event | category | flops | bytes accessed | tf_op | source)
XLA Modules:
  0.0 14.5 jit_solution(12257205608115425727)
XLA Ops:
  0.6 0.0 copy-start
  0.6 0.0 copy-start.2
  0.7 0.0 copy-start.1
  0.7 12.5 %flood_gradient.1 = f32[256,256]{1,0:T(8,128)S(1)} custom-call(f32[3,256,256]{2,1,0:T(8,128)} %water.1, f32[256,256]{1,0:T(8,128)} %ground.1, f32[256,256]{1,0:T(8,128)} %rough.1, s32[2,2]{1,0:T(2,128)} %wet_tiles.1, f32[3,256,256]{2,1,0:T(8,128)} %cot.1), custom_call_target="tpu_custom_call" | custom-call | tf_op jit(solution)/shard_map/flood_gradient/pallas_call | solution.py:497
  13.2 0.0 copy-done
  13.2 0.0 copy-done.2
  13.2 0.0 copy-done.1
  13.2 1.3 %multiply_subtract_fusion = (f32[256,256]{1,0:T(8,128)}, f32[256,256]{1,0:T(8,128)}, f32[256,256]{1,0:T(8,128)}) fusion(f32[256,256]{1,0:T(8,128)S(1)} %copy-done, f32[256,256]{1,0:T(8,128)S(1)} %flood_gradient.1, f32[256,256]{1,0:T(8,128)S(1)} %copy-done.1, f32[256,256]{1,0:T(8,128)S(1)} %copy-done.2), kind=kLoop, calls=%fused_computation.2 | loop fusion | flops 720896 | bytes 1835008 | tf_op jit(solution)/shard_map/sub | solution.py:535
Async XLA Ops:
  0.6 12.6 %copy-start = (f32[256,256]{1,0:T(8,128)S(1)}, f32[256,256]{1,0:T(8,128)}, u32[]{:S(2)}) copy-start(f32[256,256]{1,0:T(8,128)} %rough.1) | copy-start | bytes 786436
  0.6 12.6 %copy-start.2 = (f32[256,256]{1,0:T(8,128)S(1)}, f32[256,256]{1,0:T(8,128)}, u32[]{:S(2)}) copy-start(f32[256,256]{1,0:T(8,128)} %param.11) | copy-start | bytes 786436
  0.7 12.6 %copy-start.1 = (f32[256,256]{1,0:T(8,128)S(1)}, f32[256,256]{1,0:T(8,128)}, u32[]{:S(2)}) copy-start(f32[256,256]{1,0:T(8,128)} %param.10) | copy-start | bytes 786436
